TPU v7x, 128 devices: a whole 4x4x4 slice. The times are simulated.
128 devices in a mesh: ja: 8 (over x, core), ka: 16 (over z, y).
Axes of the slice: x: 4, y: 4, z: 4, core: 2. Of those that a mesh axis runs over, the one named last changes fastest.
Arguments:
- blocks: bfloat16 [512, 128, 128, 128], P(('ja', 'ka')), may hold values from -6 to 6
- coords: int32 [512, 3], P(('ja', 'ka')), may hold values from 0 to 127, as said below
- live_counts: int32 [128], P(('ja', 'ka')), may hold values from 1 to 4, as said below
- mode2_factor: bfloat16 [16384, 512], P(('ja', 'ka')), may hold values from -0.52734375 to 0.52734375
- mode3_factor: bfloat16 [16384, 512], P(('ka', 'ja')), may hold values from -0.52734375 to 0.52734375
Outputs:
- mttkrp: float32 [2048, 512], P(('ja', 'ka'))
Inputs may be any that keep to these rules, and one draw needn't show every extreme that they name: `coords`: column 0 lies in 0 to 15 and favours some popular row blocks. The device at index j of ja and k of ka holds slots whose column 1 lies in j * 16 to (j + 1) * 16 - 1 and whose column 2 lies in k * 8 to (k + 1) * 8 - 1. `live_counts`: slots of a device beyond its count are dead; some device in every draw has all 4 slots live.
All inputs are finite; a program needn't handle non-finite values.
Results may differ from a plain program's by a relative error of at most 0.0003.
Values may be sent and summed in bfloat16 or wider, within the bound.
A program may use at most 64 MiB of HBM per device.

v0:
```python
import jax
import jax.numpy as jnp
from jax import lax
from jax.sharding import PartitionSpec as P

IROWS_DEV = 16


def block_product(block_cube, mode2_rows, mode3_rows):
    contracted = jnp.einsum(
        "abc,cr->abr", block_cube, mode3_rows, preferred_element_type=jnp.float32
    )
    return jnp.einsum("abr,br->ar", contracted, mode2_rows.astype(jnp.float32))


def on_device(blocks, coords, live_counts, mode2_factor, mode3_factor):
    block_edge = blocks.shape[1]
    rank_width = mode2_factor.shape[1]
    mode2_panel = lax.all_gather(mode2_factor, "ka", axis=0, tiled=True)
    mode3_panel = lax.all_gather(mode3_factor, "ja", axis=0, tiled=True)
    mode2_start = lax.axis_index("ja") * mode2_panel.shape[0]
    mode3_start = lax.axis_index("ka") * mode3_panel.shape[0]
    column_count = lax.axis_size("ja")
    within_count = lax.axis_size("ka")
    total_rows = IROWS_DEV * column_count * within_count

    def slot_rows_of(slot_index):
        block_cube = lax.dynamic_index_in_dim(blocks, slot_index, 0, keepdims=False)
        position = lax.dynamic_index_in_dim(coords, slot_index, 0, keepdims=False)
        mode2_rows = lax.dynamic_slice_in_dim(
            mode2_panel, position[1] * block_edge - mode2_start, block_edge, 0
        )
        mode3_rows = lax.dynamic_slice_in_dim(
            mode3_panel, position[2] * block_edge - mode3_start, block_edge, 0
        )
        return (block_product(block_cube, mode2_rows, mode3_rows), position[0] * block_edge)

    def add_block(slot_index, running):
        block_rows, row_start = slot_rows_of(slot_index)
        current = lax.dynamic_slice_in_dim(running, row_start, block_rows.shape[0], 0)
        return lax.dynamic_update_slice_in_dim(running, current + block_rows, row_start, 0)

    totals = jnp.zeros((total_rows, rank_width), jnp.float32)
    totals = lax.fori_loop(jnp.int32(0), live_counts[0], add_block, totals)
    owned = lax.psum_scatter(totals, ("ja", "ka"), scatter_dimension=0, tiled=True)
    return owned


def solution(mesh):
    placed = (
        P(("ja", "ka"), None, None, None),
        P(("ja", "ka"), None),
        P(("ja", "ka")),
        P(("ja", "ka"), None),
        P(("ka", "ja"), None),
    )
    return jax.shard_map(
        on_device, mesh=mesh, in_specs=placed, out_specs=P(("ja", "ka"), None), check_vma=False
    )
```

profile of v0, /device:TPU:0, one launch (start us, length us, event | category | flops | bytes accessed | tf_op | source)
XLA Modules:
  0.0 787.4 jit_solution(4829204910456181342)
XLA Ops:
  6.5 0.0 all-gather.5.cloned.1.call-start
  6.5 0.7 all-gather.5.cloned.1.call-update
  7.3 0.0 all-gather.3.cloned.1.call-start
  7.3 0.7 all-gather.3.cloned.1.call-update
  8.0 0.0 reduce-scatter.2.cloned.1.call-start
  8.1 26.8 %all-gather.5.cloned.1.call-done = bf16[1024,512]{1,0:T(8,128)(2,1)} async-done(((bf16[128,512]{1,0:T(8,128)(2,1)}), bf16[1024,512]{1,0:T(8,128)(2,1)}) %all-gather.5.cloned.1.call-update) | async-done | bytes 1048592 | tf_op jit(solution)/shard_map/all_gather | solution.py:20
  34.9 47.4 %all-gather.3.cloned.1.call-done = bf16[2048,512]{1,0:T(8,128)(2,1)} async-done(((bf16[128,512]{1,0:T(8,128)(2,1)}), bf16[2048,512]{1,0:T(8,128)(2,1)}) %all-gather.3.cloned.1.call-update) | async-done | bytes 2097168 | tf_op jit(solution)/shard_map/all_gather | solution.py:19
  82.2 2.5 broadcast_in_dim.3
  84.7 40.7 %while.10 = (s32[]{:T(128)}, f32[2048,512]{1,0:T(8,128)}, s32[]{:T(128)}, s32[4,3]{1,0:T(4,128)}, s32[]{:T(128)}, /*index=5*/bf16[2048,512]{1,0:T(8,128)(2,1)}, ...) while((s32[]{:T(128)}, f32[2048,512]{1,0:T(8,128)}, ...), condition=%wide.region_1.2_spmd, body=%wide.region_0.1_spmd.sunk | while | flops 2164326400 | bytes 6029725 | solution.py:44
  85.4 0.7 constant_dynamic-slice_fusion.2
  86.1 0.7 fusion.13
  88.7 0.9 bitcast_convert_fusion.2
  89.6 6.8 multiply_reduce_fusion.2
  96.4 1.7 fusion.14
  98.7 0.7 constant_dynamic-slice_fusion.2
  99.4 0.7 fusion.13
  102.0 0.9 bitcast_convert_fusion.2
  103.0 6.8 multiply_reduce_fusion.2
  109.7 1.7 fusion.14
  112.1 0.7 constant_dynamic-slice_fusion.2
  112.8 0.7 fusion.13
  115.4 0.9 bitcast_convert_fusion.2
  116.3 6.8 multiply_reduce_fusion.2
  123.1 1.7 fusion.14
  125.5 0.0 reduce-scatter.2.cloned.1.call-update
  125.5 655.4 %reduce-scatter.2.cloned.1.call-done = f32[16,512]{1,0:T(8,128)} async-done(((f32[2048,512]{1,0:T(8,128)}), f32[16,512]{1,0:T(8,128)}) %reduce-scatter.2.cloned.1.call-update) | async-done | bytes 32784 | tf_op jit(solution)/shard_map/reduce_scatter | solution.py:45
Async XLA Ops:
  6.5 28.4 %all-gather.5.cloned.1.call-start = ((), (), s32[]{:S(2)}) async-start(), calls=%async_computation.2 | async-start | bytes 1179648 | tf_op jit(solution)/shard_map/all_gather | solution.py:20
  7.3 75.0 %all-gather.3.cloned.1.call-start = ((), (), s32[]{:S(2)}) async-start(), calls=%async_computation.1 | async-start | bytes 2228224 | tf_op jit(solution)/shard_map/all_gather | solution.py:19
  8.0 772.9 %reduce-scatter.2.cloned.1.call-start = ((), (), s32[]{:S(2)}) async-start(), calls=%async_computation.3 | async-start | bytes 4227072 | tf_op jit(solution)/shard_map/reduce_scatter | solution.py:45
Sparse Core Ops, SparseCore 0:
  9.1 25.7 all-gather.4
  37.0 45.1 all-gather.2
  125.6 655.2 reduce-scatter.1
where the time goes:
time: 788 us; the launch traced here: 787 us
  waiting for transfers between devices  731 us (93%)
  matrix products  20.3 us (3%)
  between operations  13.1 us (2%)
  loops' own time  8.53 us (1%)
  other arithmetic  7.89 us (1%)
    reduce_scatter x1, waiting for transfers between devices, on_device(): lax.psum_scatter(totals, ('ja', 'ka'), scatter_dimension=0, tiled=True)  655 us
    all_gather x1, waiting for transfers between devices, on_device(): mode2_panel = lax.all_gather(mode2_factor, 'ka', axis=0, tiled=True)  47.4 us
    all_gather x1, waiting for transfers between devices, on_device(): mode3_panel = lax.all_gather(mode3_factor, 'ja', axis=0, tiled=True)  26.8 us
    dot_general x3, matrix products, block_product(): jnp.einsum('abc,cr->abr', block_cube, mode3_rows, preferred_element_type=...  20.3 us
  transfers between devices with their start and end apart: 3, of which 3 were waited for; matrix products, arithmetic and copies ran while one was open for 0% of the time, Pallas kernels for 0%

commit v1 on v0

v1 whole, which is shorter than its diff:
```python
import functools

import jax
import jax.numpy as jnp
from jax import lax
from jax.experimental import pallas as pl
from jax.experimental.pallas import tpu as pltpu
from jax.sharding import PartitionSpec as P

MESH = pl.DeviceIdType.MESH

BS = 128
R = 512
SLOTS = 4
HALVES = 2
HC = R // HALVES
PHASES = 4
GROUPS = 2
TILES = 4
STEPS_PHASE = SLOTS * (8 // TILES)
SPACING = 3

GATHER2 = (("ya", "za", "yb", "zb"), ("za", "yb", "zb", "ya"), ("yb", "zb", "ya", "za"), ("zb", "ya", "za", "yb"))
GATHER3 = (("xa", "xb"), ("xb", "xa"))
SCATTER = (("xa", "ya", "za", "xb", "yb", "zb"), ("zb", "xb", "yb", "za", "xa", "ya"))
REDUCE_STEPS = 6
OFFSETS = (0, 32, 48, 56, 60, 62)


def flip_a(v, bit=1):
    return v + bit * (1 - 2 * (v % 2))


def flip_b(v, bit=1):
    return v + bit * (3 - 2 * v)


def place():
    ja = lax.axis_index("ja")
    ka = lax.axis_index("ka")
    return ja // 2, ja % 2, ka // 4, ka % 4


def partner(link):
    x, core, z, y = place()
    if link == "c":
        core = 1 - core
    elif link == "xa":
        x = flip_a(x)
    elif link == "xb":
        x = flip_b(x)
    elif link == "ya":
        y = flip_a(y)
    elif link == "yb":
        y = flip_b(y)
    elif link == "za":
        z = flip_a(z)
    else:
        z = flip_b(z)
    return (x * 2 + core, z * 4 + y)


def differing(v, w):
    low = (v + w) % 2
    high = (v // 2 + w // 2) % 2
    return (low + high) % 2, high


def kernel(
    blocks_ref, coords_ref, live_ref, mode2_ref, mode3_ref, out_ref,
    x_ref, p2a_ref, p2b_ref, p3a_ref, p3b_ref, w_ref, m_ref, rows_ref, meta_ref, sum_ref, got_ref,
    x_sem, send2, recv2, send3, recv3, send_meta, recv_meta, send_rows, recv_rows, send_sum, recv_sum,
):
    x, core, z, y = place()
    p2 = (p2a_ref, p2b_ref)
    p3 = (p3a_ref, p3b_ref)

    def block_copy(s):
        return pltpu.make_async_copy(blocks_ref.at[s], x_ref.at[s], x_sem.at[s])

    for s in range(SLOTS):
        block_copy(s).start()

    barrier = pltpu.get_barrier_semaphore()
    links = ("c", "xa", "xb", "ya", "yb", "za", "zb")
    for link in links:
        pl.semaphore_signal(barrier, inc=1, device_id=partner(link), device_id_type=MESH)

    for h in range(HALVES):
        for g in range(4):
            p2[h][g, 0] = mode2_ref[32 * g : 32 * (g + 1), HC * h : HC * (h + 1)]
        for g in range(2):
            p3[h][g, 0, 0] = mode3_ref[64 * g : 64 * (g + 1), HC * h : HC * (h + 1)]
    for s in range(SLOTS):
        mark = jnp.where(live_ref[0] > s, coords_ref[s, 0], -1).astype(jnp.float32)
        meta_ref[s] = jnp.full((8, 128), mark, jnp.float32)

    pl.semaphore_wait(barrier, len(links))

    def gather2(h, g, k):
        n = 1 << k
        return pltpu.make_async_remote_copy(
            src_ref=p2[h].at[g, pl.ds(0, n)], dst_ref=p2[h].at[g, pl.ds(n, n)],
            send_sem=send2.at[h, g, k], recv_sem=recv2.at[h, g, k],
            device_id=partner(GATHER2[g][k]), device_id_type=MESH,
        )

    def gather3(h, g, k):
        if k < 2:
            n = 1 << k
            src, dst = p3[h].at[g, 0, pl.ds(0, n)], p3[h].at[g, 0, pl.ds(n, n)]
            link = GATHER3[g][k]
        else:
            src, dst, link = p3[h].at[g, 0], p3[h].at[g, 1], "c"
        return pltpu.make_async_remote_copy(
            src_ref=src, dst_ref=dst, send_sem=send3.at[h, g, k], recv_sem=recv3.at[h, g, k],
            device_id=partner(link), device_id_type=MESH,
        )

    meta_copy = pltpu.make_async_remote_copy(
        src_ref=meta_ref.at[pl.ds(0, SLOTS)], dst_ref=meta_ref.at[pl.ds(SLOTS, SLOTS)],
        send_sem=send_meta, recv_sem=recv_meta, device_id=partner("c"), device_id_type=MESH,
    )

    for k in range(4):
        for h in range(HALVES):
            for g in range(4):
                if k > 0:
                    gather2(h, g, k - 1).wait_recv()
                gather2(h, g, k).start()
            if k < 3:
                for g in range(2):
                    if k > 0:
                        gather3(h, g, k - 1).wait_recv()
                    gather3(h, g, k).start()
    meta_copy.start()
    for s in range(SLOTS):
        block_copy(s).wait()

    def take_factors(h):
        for g in range(4):
            gather2(h, g, 3).wait_recv()
        for g in range(2):
            gather3(h, g, 2).wait_recv()
        for s in range(SLOTS):
            j = coords_ref[s, 1] % 16
            za, zb = differing(z, j // 4)
            ya, yb = differing(y, j % 4)
            bits = {"za": za, "zb": zb, "ya": ya, "yb": yb}
            for g in range(4):
                at = sum(bits[link] * (1 << k) for k, link in enumerate(GATHER2[g]))
                m_ref[s, 32 * g : 32 * (g + 1), :] = p2[h][g, at].astype(jnp.float32)
            i = coords_ref[s, 2] % 8
            xa, xb = differing(x, i // 2)
            other = (core + i % 2) % 2
            bits = {"xa": xa, "xb": xb}
            for g in range(2):
                at = sum(bits[link] * (1 << k) for k, link in enumerate(GATHER3[g]))
                w_ref[s, 64 * g : 64 * (g + 1), :] = p3[h][g, other, at]

    def rows_copy(phase, s):
        return pltpu.make_async_remote_copy(
            src_ref=rows_ref.at[phase, s], dst_ref=rows_ref.at[phase, SLOTS + s],
            send_sem=send_rows.at[phase, s], recv_sem=recv_rows.at[phase, s],
            device_id=partner("c"), device_id_type=MESH,
        )

    def compute(step):
        phase = step // STEPS_PHASE
        within = step % STEPS_PHASE
        s = within // (8 // TILES)
        first = (within % (8 // TILES)) * TILES
        for tile in range(TILES):
            u = first + tile
            lhs = x_ref[s, pl.ds(u * 16 + (phase % 2) * 8, 8)].reshape(8 * BS, BS)
            c = jnp.dot(lhs, w_ref[s], preferred_element_type=jnp.float32)
            c = (c.reshape(8, 16, 8, HC) * m_ref[s].reshape(1, 16, 8, HC)).sum(axis=1)
            rows_ref[phase, s, u] = c.sum(axis=1)

        @pl.when(within % (8 // TILES) == 8 // TILES - 1)
        def _():
            rows_copy(phase, s).start()

    def sum_copy(phase, g, k):
        n = 32 >> k
        return pltpu.make_async_remote_copy(
            src_ref=sum_ref.at[phase, g, pl.ds(n, n)], dst_ref=got_ref.at[phase, g, pl.ds(OFFSETS[k], n)],
            send_sem=send_sum.at[phase, g, k], recv_sem=recv_sum.at[phase, g, k],
            device_id=partner(SCATTER[g][k]), device_id_type=MESH,
        )

    def build(phase, g, upper):
        outer = [link for link in ("xa", "xb", "zb") if link != SCATTER[g][0]]
        weight = {link: 32 >> k for k, link in enumerate(SCATTER[g])}

        def one(m, _):
            bits = {SCATTER[g][0]: upper, outer[0]: m % 2, outer[1]: m // 2}
            x_to = flip_b(flip_a(x, bits["xa"]), bits["xb"])
            z_half = flip_b(z, bits["zb"])
            block = (x_to * 4 + core * 2 + z_half // 2).astype(jnp.float32)
            hits = [meta_ref[s] == block for s in range(2 * SLOTS)]
            base = sum(bits[link] * weight[link] for link in ("xa", "xb", "zb"))
            for za in range(2):
                z_to = flip_a(z_half, za)
                for yb in range(2):
                    for ya in range(2):
                        y_to = flip_b(flip_a(y, ya), yb)
                        u = (z_to % 2) * 4 + y_to
                        total = None
                        for s in range(2 * SLOTS):
                            term = jnp.where(hits[s], rows_ref[phase, s, u, :, 128 * g : 128 * (g + 1)], 0.0)
                            total = term if total is None else total + term
                        sum_ref[phase, g, base + za * weight["za"] + yb * weight["yb"] + ya * weight["ya"]] = total
            return 0

        lax.fori_loop(0, 4, one, 0)

    def event(e, phase):
        if e == 0:
            for s in range(SLOTS):
                rows_copy(phase, s).wait_recv()
            for g in range(GROUPS):
                build(phase, g, 1)
                sum_copy(phase, g, 0).start()
            for g in range(GROUPS):
                build(phase, g, 0)
            return
        n = 32 >> e
        for g in range(GROUPS):
            sum_copy(phase, g, e - 1).wait_recv()
            at = OFFSETS[e - 1]
            sum_ref[phase, g, n : 2 * n] = sum_ref[phase, g, n : 2 * n] + got_ref[phase, g, at + n : at + 2 * n]
            sum_copy(phase, g, e).start()
        for g in range(GROUPS):
            at = OFFSETS[e - 1]
            sum_ref[phase, g, 0:n] = sum_ref[phase, g, 0:n] + got_ref[phase, g, at : at + n]

    def one_step(step, _):
        for h in range(HALVES):
            @pl.when(step == h * 2 * STEPS_PHASE)
            def _():
                take_factors(h)
                if h == 0:
                    meta_copy.wait_recv()

        @pl.when(step < PHASES * STEPS_PHASE)
        def _():
            compute(step)

        for e in reversed(range(REDUCE_STEPS)):
            first = STEPS_PHASE + SPACING * e - 1
            after = step - first

            @pl.when((after >= 0) & (after < PHASES * STEPS_PHASE) & ((step + 8 * STEPS_PHASE - first) % STEPS_PHASE == 0))
            def _():
                event(e, (step + 8 * STEPS_PHASE - first) // STEPS_PHASE - 8)

        return 0

    total_steps = STEPS_PHASE * PHASES + SPACING * (REDUCE_STEPS - 1)
    lax.fori_loop(0, total_steps, one_step, 0)

    for phase in range(PHASES):
        for g in range(GROUPS):
            sum_copy(phase, g, REDUCE_STEPS - 1).wait_recv()
            h, t = phase // 2, phase % 2
            out_ref[8 * t : 8 * (t + 1), HC * h + 128 * g : HC * h + 128 * (g + 1)] = (
                sum_ref[phase, g, 0] + got_ref[phase, g, OFFSETS[-1]]
            )

    meta_copy.wait_send()
    for h in range(HALVES):
        for k in range(4):
            for g in range(4):
                gather2(h, g, k).wait_send()
        for k in range(3):
            for g in range(2):
                gather3(h, g, k).wait_send()

    def finish(phase, _):
        for s in range(SLOTS):
            rows_copy(phase, s).wait_send()
        for g in range(GROUPS):
            for k in range(REDUCE_STEPS):
                sum_copy(phase, g, k).wait_send()
        return 0

    lax.fori_loop(0, PHASES, finish, 0)


def on_device(blocks, coords, live_counts, mode2_factor, mode3_factor):
    dma = pltpu.SemaphoreType.DMA
    return pl.pallas_call(
        kernel,
        out_shape=jax.ShapeDtypeStruct((16, R), jnp.float32),
        in_specs=[
            pl.BlockSpec(memory_space=pl.ANY),
            pl.BlockSpec(memory_space=pltpu.SMEM),
            pl.BlockSpec(memory_space=pltpu.SMEM),
            pl.BlockSpec(memory_space=pltpu.VMEM),
            pl.BlockSpec(memory_space=pltpu.VMEM),
        ],
        out_specs=pl.BlockSpec(memory_space=pltpu.VMEM),
        scratch_shapes=[
            pltpu.VMEM((SLOTS, BS, BS, BS), jnp.bfloat16),
            pltpu.VMEM((4, 16, 32, HC), jnp.bfloat16),
            pltpu.VMEM((4, 16, 32, HC), jnp.bfloat16),
            pltpu.VMEM((2, 2, 4, 64, HC), jnp.bfloat16),
            pltpu.VMEM((2, 2, 4, 64, HC), jnp.bfloat16),
            pltpu.VMEM((SLOTS, BS, HC), jnp.bfloat16),
            pltpu.VMEM((SLOTS, BS, HC), jnp.float32),
            pltpu.VMEM((PHASES, 2 * SLOTS, 8, 8, HC), jnp.float32),
            pltpu.VMEM((2 * SLOTS, 8, 128), jnp.float32),
            pltpu.VMEM((PHASES, GROUPS, 64, 8, 128), jnp.float32),
            pltpu.VMEM((PHASES, GROUPS, 64, 8, 128), jnp.float32),
            dma((SLOTS,)),
            dma((HALVES, 4, 4)),
            dma((HALVES, 4, 4)),
            dma((HALVES, 2, 3)),
            dma((HALVES, 2, 3)),
            dma,
            dma,
            dma((PHASES, SLOTS)),
            dma((PHASES, SLOTS)),
            dma((PHASES, GROUPS, REDUCE_STEPS)),
            dma((PHASES, GROUPS, REDUCE_STEPS)),
        ],
        compiler_params=pltpu.CompilerParams(
            collective_id=0, has_side_effects=True, vmem_limit_bytes=48 * 2**20
        ),
        name="mttkrp",
    )(blocks, coords, live_counts, mode2_factor, mode3_factor)


def solution(mesh):
    placed = (
        P(("ja", "ka"), None, None, None),
        P(("ja", "ka"), None),
        P(("ja", "ka")),
        P(("ja", "ka"), None),
        P(("ka", "ja"), None),
    )
    return jax.shard_map(
        on_device, mesh=mesh, in_specs=placed, out_specs=P(("ja", "ka"), None), check_vma=False
    )
```

time: 788 us -> 91.7 us (0.12)
  waiting for transfers between devices: 731 us -> 0 us
  Pallas kernels: 0 us -> 87.7 us
  matrix products: 20.3 us -> 0 us
  between operations: 13.1 us -> 0.67 us
  loops' own time: 8.53 us -> 0 us
  other arithmetic: 7.89 us -> 0 us
    reduce_scatter x1 -> x0, waiting for transfers between devices: 655 us -> none  [on_device(): lax.psum_scatter(totals, ('ja', 'ka'), scatter_dimension=0, tiled=True)]
    pallas_call x0 -> x1, Pallas kernels: none -> 87.7 us  [on_device(): pl.pallas_call(kernel, out_shape=jax.ShapeDtypeStruct((16, R), jnp.float3...]
    all_gather x2 -> x0, waiting for transfers between devices: 74.2 us -> none  [the longest x1 47.4 us: on_device(): mode2_panel = lax.all_gather(mode2_factor, 'ka', axis=0, tiled=True)]
    dot_general x3 -> x0, matrix products: 20.3 us -> none  [block_product(): jnp.einsum('abc,cr->abr', block_cube, mode3_rows, preferred_element_type=...]
    another operation x1 -> x0, loops' own time: 8.53 us -> none  [on_device(): totals = lax.fori_loop(jnp.int32(0), live_counts[0], add_block, totals)]
  transfers between devices with their start and end apart: 3 -> 0, of which waited for: 3 -> 0; matrix products, arithmetic and copies ran while one was open for 0% -> 0% of each run, Pallas kernels for 0% -> 0%
where the time goes in v1:
time: 91.7 us; the launch traced here: 91.5 us
  Pallas kernels  87.7 us (96%)
  local copies, waits for them, and re-layouts  3.1 us (3%)
    pallas_call x1, Pallas kernels, on_device(): pl.pallas_call(kernel, out_shape=jax.ShapeDtypeStruct((16, R), jnp.float3...  87.7 us
    unnamed x7, local copies, waits for them, and re-layouts  3.1 us

profile of v1, /device:TPU:0, one launch (start us, length us, event | category | flops | bytes accessed | tf_op | source)
XLA Modules:
  0.0 91.5 jit_solution(2367608059625643977)
XLA Ops:
  0.7 0.0 copy-start
  0.7 0.9 copy-done
  1.6 0.0 copy-start.1
  1.6 0.9 copy-done.1
  2.5 0.0 copy-start.2
  2.5 0.7 copy-done.2
  3.1 87.7 %mttkrp.1 = f32[16,512]{1,0:T(8,128)S(1)} custom-call(bf16[4,128,128,128]{3,2,1,0:T(8,128)(2,1)} %blocks_ref.1, s32[4,3]{1,0:T(4,128)S(1)} %copy-done.2, s32[1]{0:T(128)S(6)} %copy.7.live_ref, bf16[128,512]{1,0:T(8,128)(2,1)S(1)} %copy-done, bf16[128,512]{1,0:T(8,128)(2,1)S(1)} %copy-done.1), custom_call_target="tpu_custom_call" | custom-call | tf_op jit(solution)/shard_map/mttkrp/pallas_call | solution.py:293
  90.9 0.6 copy.8
Async XLA Ops:
  0.7 0.9 copy-start
  1.6 0.9 copy-start.1
  2.5 0.7 copy-start.2

commit v2 on v0

v2 whole, which is shorter than its diff:
```python
import functools

import jax
import jax.numpy as jnp
from jax import lax
from jax.experimental import pallas as pl
from jax.experimental.pallas import tpu as pltpu
from jax.sharding import PartitionSpec as P

MESH = pl.DeviceIdType.MESH

BS = 128
R = 512
SLOTS = 4
HALVES = 2
HC = R // HALVES
PHASES = 4
GROUPS = 2
TILES = 4
EVENTS = ((2, 2, 2), (1, 2, 0), (0, 1, 1))
LEFT = ((1, 2), (0, 3), (2, 2), (1, 3), (2, 3))
GATHER_SLOTS = (0, 3)

GATHER2 = ("yz", "zy")
SCATTER = ("xyz", "zxy")
REDUCE_STEPS = 3
OFFSETS = (0, 48, 60)
RINGS = ("x1", "x2", "x3", "y1", "y2", "y3", "z1", "z2", "z3")


def place():
    ja = lax.axis_index("ja")
    ka = lax.axis_index("ka")
    return ja // 2, ja % 2, ka // 4, ka % 4


def partner_of(link, x, core, z, y):
    if link == "c":
        core = 1 - core
    else:
        up = int(link[1])
        if link[0] == "x":
            x = (x + up) % 4
        elif link[0] == "y":
            y = (y + up) % 4
        else:
            z = (z + up) % 4
    return (x * 2 + core, z * 4 + y)


def kernel(
    blocks_ref, coords_hbm, live_hbm, mode2_ref, mode3_ref, out_ref,
    coords_ref, live_ref, x_ref, p2a_ref, p2b_ref, p3a_ref, p3b_ref, w_ref, m_ref, rows_ref, meta_ref, sum_ref, got_ref,
    int_sem, own2_sem, own3_sem, x_sem, send2, recv2, send3, recv3, send_meta, recv_meta, send_rows, recv_rows, send_sum, recv_sum,
):
    x, core, z, y = place()
    links = ("c",) + RINGS
    partners = {link: partner_of(link, x, core, z, y) for link in links}
    partner = partners.get
    p2 = (p2a_ref, p2b_ref)
    p3 = (p3a_ref, p3b_ref)

    def block_copy(s):
        return pltpu.make_async_copy(blocks_ref.at[s], x_ref.at[s], x_sem.at[s])

    barrier = pltpu.get_barrier_semaphore()
    for link in links:
        pl.semaphore_signal(barrier, inc=1, device_id=partner(link), device_id_type=MESH)

    fetches = [
        pltpu.make_async_copy(coords_hbm, coords_ref, int_sem.at[0]),
        pltpu.make_async_copy(live_hbm, live_ref, int_sem.at[1]),
    ]

    def own2(h, g):
        return mode2_ref.at[pl.ds(64 * g, 64), pl.ds(HC * h, HC)]

    def own3(h):
        return mode3_ref.at[:, pl.ds(HC * h, HC)]

    own_copies = []
    for h in range(HALVES):
        for g in range(2):
            own_copies.append(pltpu.make_async_copy(own2(h, g), p2[h].at[g, 0, 0], own2_sem.at[h, g]))
        own_copies.append(pltpu.make_async_copy(own3(h), p3[h].at[0, 0], own3_sem.at[h]))
    for copy in fetches + own_copies:
        copy.start()

    def gather2(h, g, k, up):
        if k == 0:
            src, dst = own2(h, g), p2[h].at[g, 0, up]
        else:
            src, dst = p2[h].at[g, 0], p2[h].at[g, up]
        return pltpu.make_async_remote_copy(
            src_ref=src, dst_ref=dst, send_sem=send2.at[h, g, k, up - 1], recv_sem=recv2.at[h, g, k, up - 1],
            device_id=partner(GATHER2[g][k] + str(up)), device_id_type=MESH,
        )

    def gather3(h, up):
        if up > 0:
            src, dst, link = own3(h), p3[h].at[0, up], "x" + str(up)
        else:
            src, dst, link = p3[h].at[0], p3[h].at[1], "c"
        return pltpu.make_async_remote_copy(
            src_ref=src, dst_ref=dst, send_sem=send3.at[h, up], recv_sem=recv3.at[h, up],
            device_id=partner(link), device_id_type=MESH,
        )

    def gather_step(h, k):
        if k == 1:
            for g in range(2):
                for up in (1, 3, 2):
                    gather2(h, g, 0, up).wait_recv()
                for up in (2, 1, 3):
                    gather2(h, g, 1, up).start()
            for up in (1, 3, 2):
                gather3(h, up).wait_recv()
            gather3(h, 0).start()
            return
        for up in (2, 1, 3):
            for g in range(2):
                gather2(h, g, 0, up).start()
            gather3(h, up).start()

    pl.semaphore_wait(barrier, len(links))
    gather_step(0, 0)
    for s in range(SLOTS):
        block_copy(s).start()
    for copy in fetches + own_copies:
        copy.wait()
    for s in range(SLOTS):
        mark = jnp.where(live_ref[0] > s, coords_ref[s, 0], -1).astype(jnp.float32)
        meta_ref[s] = jnp.full((8, 128), mark, jnp.float32)

    meta_copy = pltpu.make_async_remote_copy(
        src_ref=meta_ref.at[pl.ds(0, SLOTS)], dst_ref=meta_ref.at[pl.ds(SLOTS, SLOTS)],
        send_sem=send_meta, recv_sem=recv_meta, device_id=partner("c"), device_id_type=MESH,
    )

    meta_copy.start()
    gather_step(0, 1)
    for s in range(SLOTS):
        block_copy(s).wait()

    def take_factors(h):
        for g in range(2):
            for up in (1, 3, 2):
                gather2(h, g, 1, up).wait_recv()
        gather3(h, 0).wait_recv()
        for s in range(SLOTS):
            j = coords_ref[s, 1] % 16
            back = {"z": (z - j // 4 + 4) % 4, "y": (y - j % 4 + 4) % 4}
            for g in range(2):
                first, second = GATHER2[g]
                m_ref[s, 64 * g : 64 * (g + 1), :] = p2[h][g, back[second], back[first]].astype(jnp.float32)
            i = coords_ref[s, 2] % 8
            w_ref[s] = p3[h][(core + i % 2) % 2, (x - i // 2 + 4) % 4]

    def rows_copy(phase, s):
        return pltpu.make_async_remote_copy(
            src_ref=rows_ref.at[phase, s], dst_ref=rows_ref.at[phase, SLOTS + s],
            send_sem=send_rows.at[phase, s], recv_sem=recv_rows.at[phase, s],
            device_id=partner("c"), device_id_type=MESH,
        )

    def compute(phase, s):
        def tiles(part, _):
            for tile in range(TILES):
                u = part * TILES + tile
                lhs = x_ref[s, pl.ds(u * 16 + (phase % 2) * 8, 8)].reshape(8 * BS, BS)
                c = jnp.dot(lhs, w_ref[s], preferred_element_type=jnp.float32)
                c = (c.reshape(8, 16, 8, HC) * m_ref[s].reshape(1, 16, 8, HC)).sum(axis=1)
                rows_ref[phase, s, u] = c.sum(axis=1)
            return 0

        lax.fori_loop(0, 8 // TILES, tiles, 0)
        rows_copy(phase, s).start()

    def sum_copy(phase, g, k, up):
        n = 16 >> (2 * k)
        return pltpu.make_async_remote_copy(
            src_ref=sum_ref.at[phase, g, pl.ds(n * up, n)],
            dst_ref=got_ref.at[phase, g, pl.ds(OFFSETS[k] + n * (up - 1), n)],
            send_sem=send_sum.at[phase, g, k, up - 1], recv_sem=recv_sum.at[phase, g, k, up - 1],
            device_id=partner(SCATTER[g][k] + str(up)), device_id_type=MESH,
        )

    def build(phase, g, up):
        first = SCATTER[g][0]
        weight = {axis: 16 >> (2 * k) for k, axis in enumerate(SCATTER[g])}

        def one(m, _):
            x_up, z_up = (up, m) if first == "x" else (m, up)
            z_to = (z + z_up) % 4
            block = (((x + x_up) % 4) * 4 + core * 2 + z_to // 2).astype(jnp.float32)
            hits = [meta_ref[s] == block for s in range(2 * SLOTS)]
            base = x_up * weight["x"] + z_up * weight["z"]
            for y_up in range(4):
                u = (z_to % 2) * 4 + (y + y_up) % 4
                total = None
                for s in range(2 * SLOTS):
                    term = jnp.where(hits[s], rows_ref[phase, s, u, :, 128 * g : 128 * (g + 1)], 0.0)
                    total = term if total is None else total + term
                sum_ref[phase, g, base + y_up * weight["y"]] = total
            return 0

        lax.fori_loop(0, 4, one, 0)

    def event(e, phase):
        if e == 0:
            for s in range(SLOTS):
                rows_copy(phase, s).wait_recv()
            for up in (2, 1, 3):
                for g in range(GROUPS):
                    build(phase, g, up)
                    sum_copy(phase, g, 0, up).start()
            for g in range(GROUPS):
                build(phase, g, 0)
            return
        n = 64 >> (2 * e)
        for g in range(GROUPS):
            for up in (1, 3, 2):
                sum_copy(phase, g, e - 1, up).wait_recv()
            at = OFFSETS[e - 1]

            def added(low, high):
                total = sum_ref[phase, g, low:high]
                for part in range(3):
                    total = total + got_ref[phase, g, at + part * n + low : at + part * n + high]
                sum_ref[phase, g, low:high] = total

            added(n // 4, n)
            for up in (2, 1, 3):
                sum_copy(phase, g, e, up).start()
            added(0, n // 4)

    def finish_sum(phase):
        h, t = phase // 2, phase % 2
        for g in range(GROUPS):
            for up in (1, 3, 2):
                sum_copy(phase, g, REDUCE_STEPS - 1, up).wait_recv()
            total = sum_ref[phase, g, 0]
            for part in range(3):
                total = total + got_ref[phase, g, OFFSETS[-1] + part]
            out_ref[8 * t : 8 * (t + 1), HC * h + 128 * g : HC * h + 128 * (g + 1)] = total

    def one_phase(phase, _):
        for h in range(HALVES):
            @pl.when(phase == 2 * h)
            def _():
                take_factors(h)
                if h == 0:
                    meta_copy.wait_recv()

        for s in range(SLOTS):
            for k, at in enumerate(GATHER_SLOTS):
                if at % SLOTS == s:
                    @pl.when(phase == at // SLOTS)
                    def _():
                        gather_step(1, k)

            for e, later, at in EVENTS:
                if at == s:
                    @pl.when(phase >= later)
                    def _():
                        event(e, phase - later)

            compute(phase, s)
        return 0

    lax.fori_loop(0, PHASES, one_phase, 0)
    for e, phase in LEFT:
        event(e, phase)
    for phase in range(PHASES):
        finish_sum(phase)

    meta_copy.wait_send()
    for h in range(HALVES):
        for up in range(1, 4):
            for k in range(2):
                for g in range(2):
                    gather2(h, g, k, up).wait_send()
        for up in range(4):
            gather3(h, up).wait_send()

    def finish(phase, _):
        for s in range(SLOTS):
            rows_copy(phase, s).wait_send()
        for g in range(GROUPS):
            for k in range(REDUCE_STEPS):
                for up in range(1, 4):
                    sum_copy(phase, g, k, up).wait_send()
        return 0

    lax.fori_loop(0, PHASES, finish, 0)


def on_device(blocks, coords, live_counts, mode2_factor, mode3_factor):
    dma = pltpu.SemaphoreType.DMA
    return pl.pallas_call(
        kernel,
        out_shape=jax.ShapeDtypeStruct((16, R), jnp.float32),
        in_specs=[
            pl.BlockSpec(memory_space=pltpu.HBM),
            pl.BlockSpec(memory_space=pltpu.HBM),
            pl.BlockSpec(memory_space=pltpu.HBM),
            pl.BlockSpec(memory_space=pltpu.HBM),
            pl.BlockSpec(memory_space=pltpu.HBM),
        ],
        out_specs=pl.BlockSpec(memory_space=pltpu.VMEM),
        scratch_shapes=[
            pltpu.SMEM((SLOTS, 3), jnp.int32),
            pltpu.SMEM((1,), jnp.int32),
            pltpu.VMEM((SLOTS, BS, BS, BS), jnp.bfloat16),
            pltpu.VMEM((2, 4, 4, 64, HC), jnp.bfloat16),
            pltpu.VMEM((2, 4, 4, 64, HC), jnp.bfloat16),
            pltpu.VMEM((2, 4, BS, HC), jnp.bfloat16),
            pltpu.VMEM((2, 4, BS, HC), jnp.bfloat16),
            pltpu.VMEM((SLOTS, BS, HC), jnp.bfloat16),
            pltpu.VMEM((SLOTS, BS, HC), jnp.float32),
            pltpu.VMEM((PHASES, 2 * SLOTS, 8, 8, HC), jnp.float32),
            pltpu.VMEM((2 * SLOTS, 8, 128), jnp.float32),
            pltpu.VMEM((PHASES, GROUPS, 64, 8, 128), jnp.float32),
            pltpu.VMEM((PHASES, GROUPS, 64, 8, 128), jnp.float32),
            dma((2,)),
            dma((HALVES, 2)),
            dma((HALVES,)),
            dma((SLOTS,)),
            dma((HALVES, 2, 2, 3)),
            dma((HALVES, 2, 2, 3)),
            dma((HALVES, 4)),
            dma((HALVES, 4)),
            dma,
            dma,
            dma((PHASES, SLOTS)),
            dma((PHASES, SLOTS)),
            dma((PHASES, GROUPS, REDUCE_STEPS, 3)),
            dma((PHASES, GROUPS, REDUCE_STEPS, 3)),
        ],
        compiler_params=pltpu.CompilerParams(
            collective_id=0, has_side_effects=True, vmem_limit_bytes=63 * 2**20
        ),
        name="mttkrp",
    )(blocks, coords, live_counts, mode2_factor, mode3_factor)


def solution(mesh):
    placed = (
        P(("ja", "ka"), None, None, None),
        P(("ja", "ka"), None),
        P(("ja", "ka")),
        P(("ja", "ka"), None),
        P(("ka", "ja"), None),
    )
    return jax.shard_map(
        on_device, mesh=mesh, in_specs=placed, out_specs=P(("ja", "ka"), None), check_vma=False
    )
```

time: 788 us -> 65.5 us (0.08)
  waiting for transfers between devices: 731 us -> 0 us
  Pallas kernels: 0 us -> 63.3 us
  matrix products: 20.3 us -> 0 us
  between operations: 13.1 us -> 0.66 us
  loops' own time: 8.53 us -> 0 us
  other arithmetic: 7.89 us -> 0 us
    reduce_scatter x1 -> x0, waiting for transfers between devices: 655 us -> none  [on_device(): lax.psum_scatter(totals, ('ja', 'ka'), scatter_dimension=0, tiled=True)]
    all_gather x2 -> x0, waiting for transfers between devices: 74.2 us -> none  [the longest x1 47.4 us: on_device(): mode2_panel = lax.all_gather(mode2_factor, 'ka', axis=0, tiled=True)]
    pallas_call x0 -> x1, Pallas kernels: none -> 63.3 us  [on_device(): pl.pallas_call(kernel, out_shape=jax.ShapeDtypeStruct((16, R), jnp.float3...]
    dot_general x3 -> x0, matrix products: 20.3 us -> none  [block_product(): jnp.einsum('abc,cr->abr', block_cube, mode3_rows, preferred_element_type=...]
    another operation x1 -> x0, loops' own time: 8.53 us -> none  [on_device(): totals = lax.fori_loop(jnp.int32(0), live_counts[0], add_block, totals)]
  transfers between devices with their start and end apart: 3 -> 0, of which waited for: 3 -> 0; matrix products, arithmetic and copies ran while one was open for 0% -> 0% of each run, Pallas kernels for 0% -> 0%
where the time goes in v2:
time: 65.5 us; the launch traced here: 65.3 us
  Pallas kernels  63.3 us (97%)
  local copies, waits for them, and re-layouts  1.38 us (2%)
  between operations  0.66 us (1%)
    pallas_call x1, Pallas kernels, on_device(): pl.pallas_call(kernel, out_shape=jax.ShapeDtypeStruct((16, R), jnp.float3...  63.3 us
    unnamed x1, local copies, waits for them, and re-layouts  1.38 us

profile of v2, /device:TPU:0, one launch (start us, length us, event | category | flops | bytes accessed | tf_op | source)
XLA Modules:
  0.0 65.3 jit_solution(13462755420006083492)
XLA Ops:
  0.7 63.3 %mttkrp.1 = f32[16,512]{1,0:T(8,128)} custom-call(bf16[4,128,128,128]{3,2,1,0:T(8,128)(2,1)} %blocks_ref.1, s32[4,3]{1,0:T(4,128)} %coords_hbm.1, s32[1]{0:T(128)S(6)} %copy.7.live_hbm, bf16[128,512]{1,0:T(8,128)(2,1)} %mode2_ref.1, bf16[128,512]{1,0:T(8,128)(2,1)} %mode3_ref.1), custom_call_target="tpu_custom_call" | custom-call | tf_op jit(solution)/shard_map/mttkrp/pallas_call | solution.py:300
  63.9 1.4 %copy.8 = f32[16,512]{1,0:T(8,128)} copy(f32[16,512]{1,0:T(8,128)} %mttkrp.1) | data formatting | bytes 65536

commit v3 on v2

--- a/solution.py
+++ b/solution.py
@@ -16,9 +16,9 @@
 HC = R // HALVES
 PHASES = 4
 GROUPS = 2
-TILES = 4
-EVENTS = ((2, 2, 2), (1, 2, 0), (0, 1, 1))
-LEFT = ((1, 2), (0, 3), (2, 2), (1, 3), (2, 3))
+TILES = 8
+EVENTS = ((2, 2, 3), (1, 2, 1), (0, 1, 2))
+LEFT = ((0, 3), (1, 2), (2, 2), (1, 3), (2, 3))
 GATHER_SLOTS = (0, 3)
 
 GATHER2 = ("yz", "zy")

time: 65.5 us -> 63.6 us (0.971)
  Pallas kernels: 63.3 us -> 61.3 us
    pallas_call x1, Pallas kernels: 63.3 us -> 61.3 us  [on_device(): pl.pallas_call(kernel, out_shape=jax.ShapeDtypeStruct((16, R), jnp.float3...]
where the time goes in v3:
time: 63.6 us; the launch traced here: 63.4 us
  Pallas kernels  61.3 us (96%)
  local copies, waits for them, and re-layouts  1.38 us (2%)
  between operations  0.66 us (1%)
    pallas_call x1, Pallas kernels, on_device(): pl.pallas_call(kernel, out_shape=jax.ShapeDtypeStruct((16, R), jnp.float3...  61.3 us
    unnamed x1, local copies, waits for them, and re-layouts  1.38 us

profile of v3, /device:TPU:0, one launch (start us, length us, event | category | flops | bytes accessed | tf_op | source)
XLA Modules:
  0.0 63.4 jit_solution(11817380769674031764)
XLA Ops:
  0.7 61.3 %mttkrp.1 = f32[16,512]{1,0:T(8,128)} custom-call(bf16[4,128,128,128]{3,2,1,0:T(8,128)(2,1)} %blocks_ref.1, s32[4,3]{1,0:T(4,128)} %coords_hbm.1, s32[1]{0:T(128)S(6)} %copy.7.live_hbm, bf16[128,512]{1,0:T(8,128)(2,1)} %mode2_ref.1, bf16[128,512]{1,0:T(8,128)(2,1)} %mode3_ref.1), custom_call_target="tpu_custom_call" | custom-call | tf_op jit(solution)/shard_map/mttkrp/pallas_call | solution.py:300
  62.0 1.4 %copy.8 = f32[16,512]{1,0:T(8,128)} copy(f32[16,512]{1,0:T(8,128)} %mttkrp.1) | data formatting | bytes 65536
